TPU v7x, 512 devices: a whole 4x4x16 slice. The times are simulated.
512 devices in a mesh: tile: 32 (over z, core), band: 4 (over x), pos: 4 (over y).
Axes of the slice: x: 4, y: 4, z: 16, core: 2. Of those that a mesh axis runs over, the one named last changes fastest.
Arguments:
- object_planes: float32 [2, 8192, 1024], P(None, 'tile', 'band'), may hold values from -6 to 6
- probe_planes: float32 [2, 2, 256, 256], replicated, may hold values from -6 to 6
- patterns: float32 [32, 4, 4, 3, 256, 256], P('tile', 'band', 'pos'), may hold values from 0.5 to 8
- offsets: int32 [32, 4, 4, 3, 2], P('tile', 'band', 'pos'), may hold values from 0 to 255, as said below
- counts: int32 [32, 4, 4], P('tile', 'band', 'pos'), may hold values from 0 to 3, as said below
Outputs:
- object_new: float32 [2, 8192, 1024], P(None, 'tile', 'band')
- probe_new: float32 [2, 2, 256, 256], replicated
Inputs may be any that keep to these rules, and one draw needn't show every extreme that they name: `offsets`: corners lie inside their tile: rows below 256, columns below 256. Only the first counts[t, b, p] slots of a device hold positions; later slots are to be ignored. `counts`: each device holds at most 3 positions; in every tile one device along pos holds exactly 3, and the 4 devices of a tile hold exactly 8 positions together.
All inputs are finite; a program needn't handle non-finite values.
Results may differ from a plain program's by a relative error of at most 0.0003.
Values sent between devices are 32-bit elements; how exact they have to be, the bound alone decides.
No kernel may reach another device: no remote copies, remote signals or barrier semaphores. Data moves between devices by JAX's collectives and lax.ppermute only.
A program may use at most 192 MiB of HBM per device.

v0:
```python
import math
import jax
import jax.numpy as jnp
from jax import lax
from jax.sharding import PartitionSpec as P

precise = lax.Precision.HIGHEST


def shifted(block, axis, distance):
    devices = range(lax.axis_size(axis))
    route = [(i - distance, i) for i in devices if i - distance in devices]
    return lax.ppermute(block, axis, route)


def dft_tables(pixels):
    indices = jnp.arange(pixels, dtype=jnp.int32)
    phase = indices[:, None] * indices[None, :] % pixels
    angle = phase.astype(jnp.float32) * (2.0 * math.pi / pixels)
    factor = 1.0 / math.sqrt(pixels)
    return (jnp.cos(angle) * factor, jnp.sin(angle) * factor)


def transform(real_part, imag_part, cosine, sine_table, direction):
    left_real = jnp.einsum(
        "ij,nmjk->nmik", cosine, real_part, precision=precise
    ) + direction * jnp.einsum("ij,nmjk->nmik", sine_table, imag_part, precision=precise)
    left_imag = jnp.einsum(
        "ij,nmjk->nmik", cosine, imag_part, precision=precise
    ) - direction * jnp.einsum("ij,nmjk->nmik", sine_table, real_part, precision=precise)
    out_real = jnp.einsum(
        "nmij,jk->nmik", left_real, cosine, precision=precise
    ) + direction * jnp.einsum("nmij,jk->nmik", left_imag, sine_table, precision=precise)
    out_imag = jnp.einsum(
        "nmij,jk->nmik", left_imag, cosine, precision=precise
    ) - direction * jnp.einsum("nmij,jk->nmik", left_real, sine_table, precision=precise)
    return (out_real, out_imag)


def on_device(object_planes, probe_planes, patterns, offsets, counts):
    pixels = probe_planes.shape[-1]
    capacity = patterns.shape[3]
    tile_rows = object_planes.shape[1]
    tile_cols = object_planes.shape[2]
    beside_cols = shifted(object_planes, "band", -1)
    widened = jnp.concatenate([object_planes, beside_cols], axis=2)
    below_rows = shifted(widened, "tile", -1)
    extended = jnp.concatenate([widened, below_rows], axis=1)
    local_count = counts.reshape(())
    frames = patterns[0, 0, 0]
    places = offsets[0, 0, 0]
    weights = (jnp.arange(capacity, dtype=jnp.int32) < local_count).astype(jnp.float32)
    slot_total = frames.shape[0]
    zero_index = jnp.int32(0)
    patches = jnp.stack(
        [
            lax.dynamic_slice(
                extended, (zero_index, places[number, 0], places[number, 1]), (2, pixels, pixels)
            )
            for number in range(slot_total)
        ]
    )
    patch_real = patches[:, 0][:, None]
    patch_imag = patches[:, 1][:, None]
    probe_real = probe_planes[0][None]
    probe_imag = probe_planes[1][None]
    wave_real = probe_real * patch_real - probe_imag * patch_imag
    wave_imag = probe_real * patch_imag + probe_imag * patch_real
    cosine, sine_table = dft_tables(pixels)
    far_real, far_imag = transform(wave_real, wave_imag, cosine, sine_table, 1.0)
    intensity = jnp.sum(far_real * far_real + far_imag * far_imag, axis=1)
    scaling = (jnp.sqrt(frames) / jnp.sqrt(intensity + 1.0))[:, None]
    back_real, back_imag = transform(
        far_real * scaling, far_imag * scaling, cosine, sine_table, -1.0
    )
    corr_real = back_real - wave_real
    corr_imag = back_imag - wave_imag
    slot_weight = weights[:, None, None]
    object_real = slot_weight * jnp.sum(probe_real * corr_real + probe_imag * corr_imag, axis=1)
    object_imag = slot_weight * jnp.sum(probe_real * corr_imag - probe_imag * corr_real, axis=1)
    probe_power = jnp.sum(probe_planes[0] ** 2 + probe_planes[1] ** 2, axis=0)
    lighting = slot_weight * probe_power[None]
    contributions = jnp.stack([object_real, object_imag, lighting], axis=1)
    plane_count = contributions.shape[1]
    running = jnp.zeros((plane_count, tile_rows + pixels, tile_cols + pixels), jnp.float32)
    for number in range(slot_total):
        corner_at = (zero_index, places[number, 0], places[number, 1])
        previous = lax.dynamic_slice(running, corner_at, (plane_count, pixels, pixels))
        running = lax.dynamic_update_slice(running, previous + contributions[number], corner_at)
    mode_weight = weights[:, None, None, None]
    numer_real = jnp.sum(mode_weight * (patch_real * corr_real + patch_imag * corr_imag), axis=0)
    numer_imag = jnp.sum(mode_weight * (patch_real * corr_imag - patch_imag * corr_real), axis=0)
    density = jnp.sum(slot_weight * (patches[:, 0] ** 2 + patches[:, 1] ** 2), axis=0)
    from_left = shifted(running[:, :, tile_cols:], "band", 1)
    column_core = running[:, :, :tile_cols].at[:, :, :pixels].add(from_left)
    from_above = shifted(column_core[:, tile_rows:, :], "tile", 1)
    tile_core = column_core[:, :tile_rows, :].at[:, :pixels, :].add(from_above)
    tile_total = lax.psum(tile_core, "pos")
    tile_light = tile_total[2]
    object_new = object_planes + tile_total[:2] / (tile_light + 1.0)
    sum_numer, sum_density = lax.psum(
        (jnp.stack([numer_real, numer_imag]), density), ("tile", "band", "pos")
    )
    probe_new = probe_planes + sum_numer / (sum_density + 1.0)
    return (object_new, probe_new)


def solution(mesh):
    in_specs = (
        P(None, "tile", "band"),
        P(),
        P("tile", "band", "pos", None, None, None),
        P("tile", "band", "pos", None, None),
        P("tile", "band", "pos"),
    )
    out_specs = (P(None, "tile", "band"), P())
    return jax.shard_map(
        on_device, mesh=mesh, in_specs=in_specs, out_specs=out_specs, check_vma=False
    )
```

profile of v0, /device:TPU:2, one launch (start us, length us, event | category | flops | bytes accessed | tf_op | source)
XLA Modules:
  0.0 733.1 jit_solution(11217168582069033955)
XLA Ops:
  7.2 0.0 copy-start.2
  7.2 0.0 all-reduce.6.cloned.1.call-start
  7.2 8.0 %collective-permute-start = (f32[2,256,256]{2,1,0:T(8,128)}, f32[2,256,256]{2,1,0:T(8,128)S(1)}, u32[]{:S(2)}, u32[]{:S(2)}) collective-permute-start(f32[2,256,256]{2,1,0:T(8,128)} %param.13), channel_id=1, source_target_pairs={{4,0},{8,4},{12,8},{5,1},{9,5},{13,9},{6,2},{10,6},{14,10},{7,3},{... | collective-permute-start | bytes 1572872 | tf_op jit(solution)/shard_map/ppermute | solution.py:13
  15.2 1.1 constant_dynamic-update-slice_fusion.1
  16.3 6.8 collective-permute-done
  23.1 0.1 constant_dynamic-update-slice_fusion
  23.2 1.3 collective-permute-start.1
  24.5 0.6 fusion.170
  37.1 0.1 add_reduce_fusion.2
  37.2 0.1 slice_bitcast_fusion.6
  37.3 0.0 collective-permute-done.1
  37.3 1.0 fusion.63
  38.2 0.1 pad_maximum_fusion.1
  38.4 0.1 slice_bitcast_fusion.4
  38.5 1.0 copy-done
  39.5 3.7 fusion.16
  43.2 3.7 fusion.31
  46.9 4.1 fusion.8
  51.0 3.6 fusion.10
  54.6 3.7 fusion.17
  58.3 3.7 fusion.30
  62.0 3.8 fusion.20
  65.8 0.0 copy-start.7
  65.9 3.8 add_reduce_fusion.1
  69.6 0.3 bitcast_multiply_fusion.2
  69.9 3.6 fusion.36
  73.5 3.8 fusion.32
  77.3 3.6 multiply_subtract_fusion
  80.9 3.6 fusion
  84.6 4.0 fusion.2
  88.6 3.6 multiply_add_fusion
  92.2 3.9 add_subtract_fusion
  96.2 6.0 multiply_reduce_fusion.1
  102.1 0.3 bitcast_multiply_fusion.1
  102.4 0.2 pad_maximum_fusion
  102.6 1.0 slice_bitcast_fusion.2
  103.6 0.7 copy-done.4
  104.3 0.4 broadcast_in_dim.2
  104.7 10.4 %dynamic_update_slice.9 = f32[3,512,512]{2,1,0:T(8,128)S(1)} dynamic-update-slice(f32[3,512,512]{2,1,0:T(8,128)S(1)} %broadcast_in_dim.2, f32[3,256,256]{2,1,0:T(8,128)} %slice_bitcast_fusion.2, s32[]{:T(128)} %constant.88.clone.1, s32[]{:T(128)S(6)} %select_n.65, s32[]{:T(128)S(6)} %select_n.66) | dynamic-update-slice | bytes 1572868 | tf_op jit(solution)/shard_map/dynamic_update_slice | solution.py:89
  115.1 2.3 fusion.39
  117.4 10.9 %dynamic_update_slice.10 = f32[3,512,512]{2,1,0:T(8,128)S(1)} dynamic-update-slice(f32[3,512,512]{2,1,0:T(8,128)S(1)} %dynamic_update_slice.9, f32[3,256,256]{2,1,0:T(8,128)} %fusion.39, s32[]{:T(128)} %constant.88.clone.1, s32[]{:T(128)S(6)} %select_n.67, s32[]{:T(128)S(6)} %select_n.68) | dynamic-update-slice | bytes 1572868 | tf_op jit(solution)/shard_map/dynamic_update_slice | solution.py:89
  128.2 2.3 fusion.38
  130.5 10.2 %dynamic_update_slice.11 = f32[3,512,512]{2,1,0:T(8,128)S(1)} dynamic-update-slice(f32[3,512,512]{2,1,0:T(8,128)S(1)} %dynamic_update_slice.10, f32[3,256,256]{2,1,0:T(8,128)} %fusion.38, s32[]{:T(128)} %constant.88.clone.1, s32[]{:T(128)S(6)} %select_n.69, s32[]{:T(128)S(6)} %select_n.70) | dynamic-update-slice | bytes 1572868 | tf_op jit(solution)/shard_map/dynamic_update_slice | solution.py:89
  140.8 0.2 slice.130
  141.0 7.9 %collective-permute-start.2 = (f32[3,512,256]{2,1,0:T(8,128)S(1)}, f32[3,512,256]{2,1,0:T(8,128)S(1)}, u32[]{:S(2)}, u32[]{:S(2)}) collective-permute-start(f32[3,512,256]{2,1,0:T(8,128)S(1)} %slice.130), channel_id=1, source_target_pairs={{0,4},{4,8},{8,12},{1,5},{5,9},{9,13},{2,6},{6,10},{10,14},{3,7},{... | collective-permute-start | bytes 4718600 | tf_op jit(solution)/shard_map/ppermute | solution.py:13
  148.8 34.4 %collective-permute-done.2 = f32[3,512,256]{2,1,0:T(8,128)S(1)} collective-permute-done((f32[3,512,256]{2,1,0:T(8,128)S(1)}, f32[3,512,256]{2,1,0:T(8,128)S(1)}, u32[]{:S(2)}, u32[]{:S(2)}) %collective-permute-start.2) | collective-permute-done | bytes 1572896 | tf_op jit(solution)/shard_map/ppermute | solution.py:13
  183.2 0.3 slice_add_fusion
  183.5 0.1 slice.132
  183.6 2.7 collective-permute-start.3
  186.3 1.0 pad_maximum_fusion.2
  187.4 0.9 multiply_reduce_fusion.2
  188.2 0.0 all-reduce.6.cloned.1.call-update
  188.3 0.0 copy-start.3
  188.3 0.0 all-reduce.4.cloned.1.call-start
  188.3 0.0 collective-permute-done.3
  188.3 2.2 slice_add_fusion.1
  190.5 0.0 all-reduce.4.cloned.1.call-update
  190.6 472.6 %all-reduce.6.cloned.1.call-done = (f32[2,2,256,256]{3,2,1,0:T(8,128)}, f32[256,256]{1,0:T(8,128)}) async-done(((f32[2,2,256,256]{3,2,1,0:T(8,128)}, f32[256,256]{1,0:T(8,128)}), (f32[2,2,256,256]{3,2,1,0:T(8,128)}, f32[256,256]{1,0:T(8,128)})) %all-reduce.6.cloned.1.call-update) | async-done | bytes 1310736 | tf_op jit(solution)/shard_map/psum | solution.py:101
  663.2 1.0 broadcast_add_fusion
  664.2 0.0 copy-start.6
  664.2 2.4 divide_add_fusion
  666.6 56.5 %all-reduce.4.cloned.1.call-done = f32[3,256,256]{2,1,0:T(8,128)} async-done(((f32[3,256,256]{2,1,0:T(8,128)}), f32[3,256,256]{2,1,0:T(8,128)}) %all-reduce.4.cloned.1.call-update) | async-done | bytes 786448 | tf_op jit(solution)/shard_map/psum | solution.py:98
  723.1 1.0 fusion.70
  724.1 1.9 fusion.66
  (17 shorter events, 0.0 us)
Async XLA Ops:
  7.2 17.3 %copy-start.10 = (s32[1,1,1,3,2]{3,4,2,1,0:T(2,128)S(1)}, s32[1,1,1,3,2]{3,4,2,1,0:T(2,128)}, u32[]{:S(2)}) copy-start(s32[1,1,1,3,2]{3,4,2,1,0:T(2,128)} %param.16) | copy-start | bytes 76
  7.2 29.9 %copy-start.2 = (f32[2,2,256,256]{3,2,1,0:T(8,128)S(1)}, f32[2,2,256,256]{3,2,1,0:T(8,128)}, u32[]{:S(2)}) copy-start(f32[2,2,256,256]{3,2,1,0:T(8,128)} %param.14) | copy-start | bytes 3145732
  7.2 656.0 %all-reduce.6.cloned.1.call-start = ((), (), s32[]{:S(2)}) async-start(), calls=%async_computation.1 | async-start | bytes 2621440 | tf_op jit(solution)/shard_map/psum | solution.py:101
  7.2 15.9 %collective-permute-start = (f32[2,256,256]{2,1,0:T(8,128)}, f32[2,256,256]{2,1,0:T(8,128)S(1)}, u32[]{:S(2)}, u32[]{:S(2)}) collective-permute-start(f32[2,256,256]{2,1,0:T(8,128)} %param.13), channel_id=1, source_target_pairs={{4,0},{8,4},{12,8},{5,1},{9,5},{13,9},{6,2},{10,6},{14,10},{7,3},{... | collective-permute-start | bytes 1572872 | tf_op jit(solution)/shard_map/ppermute | solution.py:13
  23.2 14.1 %collective-permute-start.1 = (f32[2,256,512]{2,1,0:T(8,128)S(1)}, f32[2,256,512]{2,1,0:T(8,128)S(1)}, u32[]{:S(2)}, u32[]{:S(2)}) collective-permute-start(f32[2,256,512]{2,1,0:T(8,128)S(1)} %constant_dynamic-update-slice_fusion), channel_id=1, source_target_pairs={{16,0},{32,16},{48,32},{64,48},{80,64},{96,80},{112,96},{128,112},... | collective-permute-start | bytes 3145736 | tf_op jit(solution)/shard_map/ppermute | solution.py:13
  38.3 1.1 copy-start
  65.8 3.8 copy-start.7
  102.6 1.7 copy-start.4
  141.0 42.3 %collective-permute-start.2 = (f32[3,512,256]{2,1,0:T(8,128)S(1)}, f32[3,512,256]{2,1,0:T(8,128)S(1)}, u32[]{:S(2)}, u32[]{:S(2)}) collective-permute-start(f32[3,512,256]{2,1,0:T(8,128)S(1)} %slice.130), channel_id=1, source_target_pairs={{0,4},{4,8},{8,12},{1,5},{5,9},{9,13},{2,6},{6,10},{10,14},{3,7},{... | collective-permute-start | bytes 4718600 | tf_op jit(solution)/shard_map/ppermute | solution.py:13
  183.2 3.1 copy-start.8
  183.2 3.1 copy-start.9
  183.5 3.9 copy-start.5
  183.5 3.9 copy-start.1
  183.6 4.7 collective-permute-start.3
  188.3 475.9 %copy-start.3 = (f32[2,2,256,256]{3,2,1,0:T(8,128)S(1)}, f32[2,2,256,256]{3,2,1,0:T(8,128)}, u32[]{:S(2)}) copy-start(f32[2,2,256,256]{3,2,1,0:T(8,128)} %param.14) | copy-start | bytes 3145732
  188.3 534.9 %all-reduce.4.cloned.1.call-start = ((), (), s32[]{:S(2)}) async-start(), calls=%async_computation | async-start | bytes 1572864 | tf_op jit(solution)/shard_map/psum | solution.py:98
  664.2 59.9 %copy-start.6 = (f32[2,256,256]{2,1,0:T(8,128)S(1)}, f32[2,256,256]{2,1,0:T(8,128)}, u32[]{:S(2)}) copy-start(f32[2,256,256]{2,1,0:T(8,128)} %param.13) | copy-start | bytes 1572868
Sparse Core Ops, SparseCore 0:
  188.4 474.7 all-reduce.5
  665.6 57.5 all-reduce.3
where the time goes:
time: 743 us; the launch traced here: 733 us
  waiting for transfers between devices  570 us (77%)
  matrix products  62.2 us (8%)
  local copies, waits for them, and re-layouts  36.8 us (5%)
  between operations  26.6 us (4%)
  starting transfers between devices  19.9 us (3%)
  other arithmetic  17.1 us (2%)
    psum x1, waiting for transfers between devices, on_device(): lax.psum((jnp.stack([numer_real, numer_imag]), density), ('tile', 'band',...  473 us
    psum x1, waiting for transfers between devices, on_device(): tile_total = lax.psum(tile_core, 'pos')  56.5 us
    ppermute x4, waiting for transfers between devices, shifted(): return lax.ppermute(block, axis, route)  41.2 us
    dynamic_update_slice x3, local copies, waits for them, and re-layouts, on_device(): lax.dynamic_update_slice(running, previous + contributions[number], corne...  31.5 us
    ppermute x4, starting transfers between devices, shifted(): return lax.ppermute(block, axis, route)  19.8 us
  transfers between devices with their start and end apart: 6, of which 4 were waited for; matrix products, arithmetic and copies ran while one was open for 1% of the time, Pallas kernels for 0%

commit v1 on v0

--- a/solution.py
+++ b/solution.py
@@ -99,7 +99,7 @@
     tile_light = tile_total[2]
     object_new = object_planes + tile_total[:2] / (tile_light + 1.0)
     sum_numer, sum_density = lax.psum(
-        (jnp.stack([numer_real, numer_imag]), density), ("tile", "band", "pos")
+        lax.psum((jnp.stack([numer_real, numer_imag]), density), "tile"), ("band", "pos")
     )
     probe_new = probe_planes + sum_numer / (sum_density + 1.0)
     return (object_new, probe_new)

time: 743 us -> 576 us (0.78)
  waiting for transfers between devices: 570 us -> 403 us
    psum x1 -> x2, waiting for transfers between devices: 473 us -> 335 us  [the longest x1 220 us: on_device(): lax.psum((jnp.stack([numer_real, numer_imag]), density), 'tile')]
    ppermute x4, waiting for transfers between devices: 41.2 us -> 8.67 us  [shifted(): return lax.ppermute(block, axis, route)]
  transfers between devices with their start and end apart: 6 -> 7, of which waited for: 4 -> 5; matrix products, arithmetic and copies ran while one was open for 1% -> 2% of each run, Pallas kernels for 0% -> 0%
where the time goes in v1:
time: 576 us; the launch traced here: 566 us
  waiting for transfers between devices  403 us (70%)
  matrix products  62.2 us (11%)
  local copies, waits for them, and re-layouts  38 us (7%)
  between operations  26.2 us (5%)
  starting transfers between devices  19.6 us (3%)
  other arithmetic  17.3 us (3%)
    psum x1, waiting for transfers between devices, on_device(): lax.psum((jnp.stack([numer_real, numer_imag]), density), 'tile')  220 us
    psum x1, waiting for transfers between devices, on_device(): lax.psum(lax.psum((jnp.stack([numer_real, numer_imag]), density), 'tile')...  115 us
    psum x1, waiting for transfers between devices, on_device(): tile_total = lax.psum(tile_core, 'pos')  58.7 us
    dynamic_update_slice x3, local copies, waits for them, and re-layouts, on_device(): lax.dynamic_update_slice(running, previous + contributions[number], corne...  31.5 us
    ppermute x4, starting transfers between devices, shifted(): return lax.ppermute(block, axis, route)  19.5 us
  transfers between devices with their start and end apart: 7, of which 5 were waited for; matrix products, arithmetic and copies ran while one was open for 2% of the time, Pallas kernels for 0%

profile of v1, /device:TPU:2, one launch (start us, length us, event | category | flops | bytes accessed | tf_op | source)
XLA Modules:
  0.0 566.0 jit_solution(714760384071132590)
XLA Ops:
  7.2 0.0 all-reduce.8.cloned.1.call-start
  7.2 8.0 %collective-permute-start = (f32[2,256,256]{2,1,0:T(8,128)}, f32[2,256,256]{2,1,0:T(8,128)S(1)}, u32[]{:S(2)}, u32[]{:S(2)}) collective-permute-start(f32[2,256,256]{2,1,0:T(8,128)} %param.13), channel_id=1, source_target_pairs={{4,0},{8,4},{12,8},{5,1},{9,5},{13,9},{6,2},{10,6},{14,10},{7,3},{... | collective-permute-start | bytes 1572872 | tf_op jit(solution)/shard_map/ppermute | solution.py:13
  15.2 1.1 constant_dynamic-update-slice_fusion.1
  16.3 6.8 %collective-permute-done = f32[2,256,256]{2,1,0:T(8,128)S(1)} collective-permute-done((f32[2,256,256]{2,1,0:T(8,128)}, f32[2,256,256]{2,1,0:T(8,128)S(1)}, u32[]{:S(2)}, u32[]{:S(2)}) %collective-permute-start) | collective-permute-done | bytes 524320 | tf_op jit(solution)/shard_map/ppermute | solution.py:13
  23.1 0.1 constant_dynamic-update-slice_fusion
  23.2 1.3 collective-permute-start.1
  24.5 0.7 fusion.170
  37.0 0.1 add_reduce_fusion.2
  37.1 0.1 slice_bitcast_fusion.6
  37.2 1.0 fusion.63
  38.1 0.1 pad_maximum_fusion.1
  38.3 0.1 slice_bitcast_fusion.4
  38.4 1.0 copy-done
  39.4 3.7 fusion.16
  43.1 3.7 fusion.31
  46.8 4.1 fusion.8
  50.9 3.6 fusion.10
  54.5 3.7 fusion.17
  58.2 3.7 fusion.30
  61.9 3.8 fusion.20
  65.8 0.0 copy-start.6
  65.8 3.8 add_reduce_fusion.1
  69.6 0.3 bitcast_multiply_fusion.2
  69.8 3.6 fusion.36
  73.4 3.8 fusion.32
  77.2 3.6 multiply_subtract_fusion
  80.8 3.6 fusion
  84.5 4.0 fusion.2
  88.5 3.6 multiply_add_fusion
  92.1 3.9 add_subtract_fusion
  96.1 6.0 %multiply_reduce_fusion.1 = (f32[2,256,256]{2,1,0:T(8,128)}, f32[2,256,256]{2,1,0:T(8,128)}, f32[3,256,256]{2,1,0:T(8,128)S(1)}, f32[3,256,256]{2,1,0:T(8,128)S(1)}) fusion(f32[3,2,256,256]{3,2,1,0:T(8,128)S(1)} %add_subtract_fusion, f32[3]{0:T(128)S(1)} %compare_convert_fusion, f32[3,256,256]{2,1,0:T(8,128)S(1)} %get-tuple-element.56, ...), kind=kOutput, calls=%fused_computation.26 | convolution fusion | flops 1217724416 | bytes 9961484 | tf_op jit(solution)/shard_map/nmij,jk->nmik/dot_general | solution.py:36
  102.1 0.3 bitcast_multiply_fusion.1
  102.3 0.2 pad_maximum_fusion
  102.5 1.0 slice_bitcast_fusion.2
  103.5 0.7 copy-done.4
  104.2 0.4 broadcast_in_dim.2
  104.6 10.4 %dynamic_update_slice.9 = f32[3,512,512]{2,1,0:T(8,128)S(1)} dynamic-update-slice(f32[3,512,512]{2,1,0:T(8,128)S(1)} %broadcast_in_dim.2, f32[3,256,256]{2,1,0:T(8,128)} %slice_bitcast_fusion.2, s32[]{:T(128)} %constant.88.clone.1, s32[]{:T(128)S(6)} %select_n.65, s32[]{:T(128)S(6)} %select_n.66) | dynamic-update-slice | bytes 1572868 | tf_op jit(solution)/shard_map/dynamic_update_slice | solution.py:89
  115.0 2.3 fusion.39
  117.3 10.9 %dynamic_update_slice.10 = f32[3,512,512]{2,1,0:T(8,128)S(1)} dynamic-update-slice(f32[3,512,512]{2,1,0:T(8,128)S(1)} %dynamic_update_slice.9, f32[3,256,256]{2,1,0:T(8,128)} %fusion.39, s32[]{:T(128)} %constant.88.clone.1, s32[]{:T(128)S(6)} %select_n.67, s32[]{:T(128)S(6)} %select_n.68) | dynamic-update-slice | bytes 1572868 | tf_op jit(solution)/shard_map/dynamic_update_slice | solution.py:89
  128.1 2.3 fusion.38
  130.4 10.2 %dynamic_update_slice.11 = f32[3,512,512]{2,1,0:T(8,128)S(1)} dynamic-update-slice(f32[3,512,512]{2,1,0:T(8,128)S(1)} %dynamic_update_slice.10, f32[3,256,256]{2,1,0:T(8,128)} %fusion.38, s32[]{:T(128)} %constant.88.clone.1, s32[]{:T(128)S(6)} %select_n.69, s32[]{:T(128)S(6)} %select_n.70) | dynamic-update-slice | bytes 1572868 | tf_op jit(solution)/shard_map/dynamic_update_slice | solution.py:89
  140.7 0.0 copy-start.7
  140.7 1.3 slice.130
  142.0 8.0 %collective-permute-start.2 = (f32[3,512,256]{2,1,0:T(8,128)}, f32[3,512,256]{2,1,0:T(8,128)}, u32[]{:S(2)}, u32[]{:S(2)}) collective-permute-start(f32[3,512,256]{2,1,0:T(8,128)} %slice.130), channel_id=1, source_target_pairs={{0,4},{4,8},{8,12},{1,5},{5,9},{9,13},{2,6},{6,10},{10,14},{3,7},{... | collective-permute-start | bytes 4718600 | tf_op jit(solution)/shard_map/ppermute | solution.py:13
  150.1 1.0 pad_maximum_fusion.2
  151.1 0.9 multiply_reduce_fusion.2
  152.0 0.0 all-reduce.8.cloned.1.call-update
  152.0 0.0 all-reduce.10.cloned.1.call-start
  152.0 220.2 %all-reduce.8.cloned.1.call-done = (f32[2,2,256,256]{3,2,1,0:T(8,128)}, f32[256,256]{1,0:T(8,128)}) async-done(((f32[2,2,256,256]{3,2,1,0:T(8,128)}, f32[256,256]{1,0:T(8,128)}), (f32[2,2,256,256]{3,2,1,0:T(8,128)}, f32[256,256]{1,0:T(8,128)})) %all-reduce.8.cloned.1.call-update) | async-done | bytes 1310736 | tf_op jit(solution)/shard_map/psum | solution.py:102
  372.2 0.0 all-reduce.10.cloned.1.call-update
  372.2 0.0 all-reduce.6.cloned.1.call-start
  372.3 1.7 slice_add_fusion
  374.0 0.1 slice.132
  374.0 0.0 copy-start.3
  374.1 2.2 collective-permute-start.3
  376.3 1.8 collective-permute-done.3
  378.1 1.0 slice_add_fusion.1
  379.1 0.0 all-reduce.6.cloned.1.call-update
  379.2 115.1 %all-reduce.10.cloned.1.call-done = (f32[2,2,256,256]{3,2,1,0:T(8,128)}, f32[256,256]{1,0:T(8,128)}) async-done(((f32[2,2,256,256]{3,2,1,0:T(8,128)}, f32[256,256]{1,0:T(8,128)}), (f32[2,2,256,256]{3,2,1,0:T(8,128)}, f32[256,256]{1,0:T(8,128)})) %all-reduce.10.cloned.1.call-update) | async-done | bytes 1310736 | tf_op jit(solution)/shard_map/psum | solution.py:101
  494.2 1.0 broadcast_add_fusion
  495.2 2.4 divide_add_fusion
  497.6 58.7 %all-reduce.6.cloned.1.call-done = f32[3,256,256]{2,1,0:T(8,128)} async-done(((f32[3,256,256]{2,1,0:T(8,128)}), f32[3,256,256]{2,1,0:T(8,128)}) %all-reduce.6.cloned.1.call-update) | async-done | bytes 786448 | tf_op jit(solution)/shard_map/psum | solution.py:98
  556.3 1.0 fusion.70
  557.3 1.9 fusion.66
  (18 shorter events, 0.0 us)
Async XLA Ops:
  7.2 17.3 %copy-start.9 = (s32[1,1,1,3,2]{3,4,2,1,0:T(2,128)S(1)}, s32[1,1,1,3,2]{3,4,2,1,0:T(2,128)}, u32[]{:S(2)}) copy-start(s32[1,1,1,3,2]{3,4,2,1,0:T(2,128)} %param.16) | copy-start | bytes 76
  7.2 29.8 %copy-start.2 = (f32[2,2,256,256]{3,2,1,0:T(8,128)S(1)}, f32[2,2,256,256]{3,2,1,0:T(8,128)}, u32[]{:S(2)}) copy-start(f32[2,2,256,256]{3,2,1,0:T(8,128)} %param.14) | copy-start | bytes 3145732
  7.2 365.0 %all-reduce.8.cloned.1.call-start = ((), (), s32[]{:S(2)}) async-start(), calls=%async_computation.1 | async-start | bytes 2621440 | tf_op jit(solution)/shard_map/psum | solution.py:102
  7.2 15.9 %collective-permute-start = (f32[2,256,256]{2,1,0:T(8,128)}, f32[2,256,256]{2,1,0:T(8,128)S(1)}, u32[]{:S(2)}, u32[]{:S(2)}) collective-permute-start(f32[2,256,256]{2,1,0:T(8,128)} %param.13), channel_id=1, source_target_pairs={{4,0},{8,4},{12,8},{5,1},{9,5},{13,9},{6,2},{10,6},{14,10},{7,3},{... | collective-permute-start | bytes 1572872 | tf_op jit(solution)/shard_map/ppermute | solution.py:13
  23.2 14.0 %collective-permute-start.1 = (f32[2,256,512]{2,1,0:T(8,128)S(1)}, f32[2,256,512]{2,1,0:T(8,128)S(1)}, u32[]{:S(2)}, u32[]{:S(2)}) collective-permute-start(f32[2,256,512]{2,1,0:T(8,128)S(1)} %constant_dynamic-update-slice_fusion), channel_id=1, source_target_pairs={{16,0},{32,16},{48,32},{64,48},{80,64},{96,80},{112,96},{128,112},... | collective-permute-start | bytes 3145736 | tf_op jit(solution)/shard_map/ppermute | solution.py:13
  38.3 1.1 copy-start
  65.8 3.8 copy-start.6
  102.5 1.7 copy-start.4
  140.7 9.4 %copy-start.7 = (f32[2,256,256]{2,1,0:T(8,128)S(1)}, f32[2,256,256]{2,1,0:T(8,128)}, u32[]{:S(2)}) copy-start(f32[2,256,256]{2,1,0:T(8,128)} %get-tuple-element.42) | copy-start | bytes 1572868
  140.7 9.4 %copy-start.8 = (f32[2,256,256]{2,1,0:T(8,128)S(1)}, f32[2,256,256]{2,1,0:T(8,128)}, u32[]{:S(2)}) copy-start(f32[2,256,256]{2,1,0:T(8,128)} %get-tuple-element.43) | copy-start | bytes 1572868
  142.0 9.1 %copy-start.1 = (f32[3,2,256,256]{3,2,0,1:T(8,128)S(1)}, f32[3,2,256,256]{3,2,0,1:T(8,128)}, u32[]{:S(2)}) copy-start(f32[3,2,256,256]{3,2,0,1:T(8,128)} %copy-done) | copy-start | bytes 4718596
  142.0 230.2 %collective-permute-start.2 = (f32[3,512,256]{2,1,0:T(8,128)}, f32[3,512,256]{2,1,0:T(8,128)}, u32[]{:S(2)}, u32[]{:S(2)}) collective-permute-start(f32[3,512,256]{2,1,0:T(8,128)} %slice.130), channel_id=1, source_target_pairs={{0,4},{4,8},{8,12},{1,5},{5,9},{9,13},{2,6},{6,10},{10,14},{3,7},{... | collective-permute-start | bytes 4718600 | tf_op jit(solution)/shard_map/ppermute | solution.py:13
  152.0 342.3 %all-reduce.10.cloned.1.call-start = ((), (), s32[]{:S(2)}) async-start(), calls=%async_computation.2 | async-start | bytes 2621440 | tf_op jit(solution)/shard_map/psum | solution.py:101
  372.2 184.1 %all-reduce.6.cloned.1.call-start = ((), (), s32[]{:S(2)}) async-start(), calls=%async_computation | async-start | bytes 1572864 | tf_op jit(solution)/shard_map/psum | solution.py:98
  374.0 121.2 %copy-start.3 = (f32[2,2,256,256]{3,2,1,0:T(8,128)S(1)}, f32[2,2,256,256]{3,2,1,0:T(8,128)}, u32[]{:S(2)}) copy-start(f32[2,2,256,256]{3,2,1,0:T(8,128)} %param.14) | copy-start | bytes 3145732
  374.1 4.1 collective-permute-start.3
  495.2 62.1 %copy-start.5 = (f32[2,256,256]{2,1,0:T(8,128)S(1)}, f32[2,256,256]{2,1,0:T(8,128)}, u32[]{:S(2)}) copy-start(f32[2,256,256]{2,1,0:T(8,128)} %param.13) | copy-start | bytes 1572868
Sparse Core Ops, SparseCore 0:
  152.1 220.0 all-reduce.7
  375.9 118.3 all-reduce.9
  496.7 59.5 all-reduce.5
